TPU v7x, 32 devices: a whole 2x2x4 slice. The times are simulated.
32 devices in a mesh: dp: 8 (over y, x, core), tensor: 4 (over z).
Axes of the slice: x: 2, y: 2, z: 4, core: 2. Of those that a mesh axis runs over, the one named last changes fastest.
Arguments:
- tokens: bfloat16 [8192, 1536], P(('dp', 'tensor')), may hold values from -6 to 6
- first_gain: float32 [1536], replicated, may hold values from 0.25 to 1.75
- query_weight: bfloat16 [1536, 768], P(None, 'tensor'), may hold values from -0.0625 to 0.0625
- key_weight: bfloat16 [1536, 768], P(None, 'tensor'), may hold values from -0.0625 to 0.0625
- value_weight: bfloat16 [1536, 768], P(None, 'tensor'), may hold values from -0.15625 to 0.15625
- out_weight: bfloat16 [1536, 768], P(None, 'tensor'), may hold values from -0.875 to 0.875
- bucket_table: float32 [32, 12], P(None, 'tensor'), may hold values from -3 to 3
- second_gain: float32 [1536], replicated, may hold values from 0.25 to 1.75
- gate_weight: bfloat16 [1536, 3968], P(None, 'tensor'), may hold values from -0.15625 to 0.15625
- up_weight: bfloat16 [1536, 3968], P(None, 'tensor'), may hold values from -0.15625 to 0.15625
- down_weight: bfloat16 [1536, 3968], P(None, 'tensor'), may hold values from -0.09375 to 0.09375
- piece_start: int32 [8, 2], P('dp'), may hold values from 0 to 768, as said below
- bucket_index: int32 [2047], replicated, may hold values from 0 to 31, as said below
- cotangent: bfloat16 [8192, 1536], P(('dp', 'tensor')), may hold values from -6 to 6
Outputs:
- layer_out: bfloat16 [8192, 1536], P(('dp', 'tensor'))
- input_grad: bfloat16 [8192, 1536], P(('dp', 'tensor'))
- first_gain_grad: float32 [1536], replicated
- query_grad: float32 [1536, 768], P('dp', 'tensor')
- key_grad: float32 [1536, 768], P('dp', 'tensor')
- value_grad: float32 [1536, 768], P('dp', 'tensor')
- out_grad: float32 [1536, 768], P('dp', 'tensor')
- table_grad: float32 [32, 12], P(None, 'tensor')
- second_gain_grad: float32 [1536], replicated
- gate_grad: float32 [1536, 3968], P('dp', 'tensor')
- up_grad: float32 [1536, 3968], P('dp', 'tensor')
- down_grad: float32 [1536, 3968], P('dp', 'tensor')
Inputs may be any that keep to these rules, and one draw needn't show every extreme that they name: `piece_start`: piece p of a sequence lies within positions p * 512 to (p + 1) * 512 - 1, so pieces never intersect. bucket_index[d + 1023] is the bucket of key minus query position d: for d <= 0 it lies below 16 and equals |d| when |d| < 8; for d > 0 it is 16 plus the bucket that -d has, so it equals |d| + 32 // 2 when |d| < 8; it never falls as |d| grows on either side.
All inputs are finite; a program needn't handle non-finite values.
Results may differ from a plain program's by a relative error of at most 0.02.
Values may be sent and summed in bfloat16 or wider, within the bound.
A program may use at most 192 MiB of HBM per device.

v0:
```python
import jax
import jax.numpy as jnp
from jax import lax
from jax.sharding import PartitionSpec as P

NB = 32
LEN = 1024
QBLK = 512
PIECE = 256
NPIECE = 2
EPSILON = 1e-06
MASKED = -1000000000.0
HIGHEST = lax.Precision.HIGHEST


def normed(row_block, gain_vec):
    inv_rms = lax.rsqrt(jnp.mean(row_block * row_block, axis=-1, keepdims=True) + EPSILON)
    return row_block * inv_rms * gain_vec


def gelu_tanh(values):
    return jax.nn.gelu(values, approximate=True)


def piece_labels(starts_row, position):
    inside = (position[None, :] >= starts_row[:, None]) & (
        position[None, :] < starts_row[:, None] + PIECE
    )
    labels = jnp.arange(1, NPIECE + 1, dtype=jnp.int32)
    return jnp.sum(inside.astype(jnp.int32) * labels[:, None], axis=0) - 1


def bias_rows(distance_bias, query_start):
    width = QBLK + LEN - 1
    window = lax.dynamic_slice_in_dim(distance_bias, LEN - QBLK - query_start, width, 1)
    heads = window.shape[0]
    tiled = jnp.tile(window, (1, QBLK + 1))[:, : QBLK * (width + 1)]
    skewed = tiled.reshape(heads, QBLK, width + 1)[:, :, :LEN]
    return jnp.flip(skewed, axis=1)


def diagonal_sums(grad_block):
    width = QBLK + LEN - 1
    heads = grad_block.shape[0]
    flipped = jnp.flip(grad_block, axis=1)
    padded = jnp.pad(flipped, ((0, 0), (0, 0), (0, width + 1 - LEN)))
    flat = jnp.pad(padded.reshape(heads, QBLK * (width + 1)), ((0, 0), (0, LEN - 1)))
    return jnp.sum(flat.reshape(heads, QBLK + 1, width), axis=1)


def block_scores(query_block, key_seq, distance_bias, starts_row, query_start):
    query_pos = query_start + jnp.arange(QBLK, dtype=jnp.int32)
    key_pos = jnp.arange(LEN, dtype=jnp.int32)
    query_piece = piece_labels(starts_row, query_pos)
    key_piece = piece_labels(starts_row, key_pos)
    allowed = (key_pos[None, :] <= query_pos[:, None]) | (
        query_piece[:, None] == key_piece[None, :]
    ) & (query_piece[:, None] >= 0)
    raw_scores = jnp.einsum(
        "qhd,khd->hqk", query_block, key_seq, preferred_element_type=jnp.float32
    )
    return jnp.where(allowed[None], raw_scores + bias_rows(distance_bias, query_start), MASKED)


def locate(block_id):
    per_seq = LEN // QBLK
    sequence = block_id // per_seq
    query_start = block_id % per_seq * QBLK
    return (sequence, query_start, sequence * LEN + query_start)


def per_device(
    tokens,
    first_gain,
    query_weight,
    key_weight,
    value_weight,
    out_weight,
    bucket_table,
    second_gain,
    gate_weight,
    up_weight,
    down_weight,
    piece_start,
    bucket_index,
    cotangent,
):
    own_rows = tokens.shape[0]
    groups = piece_start.shape[0]
    all_rows = groups * LEN
    head_count = bucket_table.shape[1]
    inner_dev = query_weight.shape[1]
    head_dim = inner_dev // head_count
    block_count = all_rows // QBLK
    contract_cols = (((1,), (1,)), ((), ()))
    contract_rows = (((0,), (0,)), ((), ()))
    distance_hot = (bucket_index[:, None] == jnp.arange(NB, dtype=jnp.int32)[None, :]).astype(
        jnp.float32
    )
    distance_bias = jnp.dot(distance_hot, bucket_table, precision=HIGHEST).T
    inputs = tokens.astype(jnp.float32)
    norm_first = normed(inputs, first_gain).astype(jnp.bfloat16)
    first_all = lax.all_gather(norm_first, "tensor", axis=0, tiled=True)
    query_low = jnp.dot(first_all, query_weight, preferred_element_type=jnp.float32).astype(
        jnp.bfloat16
    )
    key_low = jnp.dot(first_all, key_weight, preferred_element_type=jnp.float32).astype(
        jnp.bfloat16
    )
    value_low = jnp.dot(first_all, value_weight, preferred_element_type=jnp.float32).astype(
        jnp.bfloat16
    )
    query_heads = query_low.reshape(all_rows, head_count, head_dim)
    key_heads = key_low.reshape(all_rows, head_count, head_dim)
    value_heads = value_low.reshape(all_rows, head_count, head_dim)

    def forward_block(block_id):
        sequence, query_start, row_start = locate(block_id)
        query_block = lax.dynamic_slice_in_dim(query_heads, row_start, QBLK, 0)
        scores = block_scores(
            query_block, key_heads, distance_bias, piece_start[sequence], query_start
        )
        peak = jnp.max(scores, axis=-1, keepdims=True)
        powered = jnp.exp(scores - peak)
        row_total = jnp.sum(powered, axis=-1, keepdims=True)
        softmax_low = (powered / row_total).astype(jnp.bfloat16)
        attended = jnp.einsum(
            "hqk,khd->qhd", softmax_low, value_heads, preferred_element_type=jnp.float32
        )
        return (attended.reshape(QBLK, inner_dev), (peak + jnp.log(row_total))[..., 0])

    attended, log_norms = lax.map(forward_block, jnp.arange(block_count, dtype=jnp.int32))
    attended_low = attended.reshape(all_rows, inner_dev).astype(jnp.bfloat16)
    picked = attended_low
    middle = inputs + lax.psum_scatter(
        lax.dot_general(
            picked, out_weight, contract_cols, preferred_element_type=jnp.float32
        ).astype(jnp.bfloat16),
        "tensor",
        scatter_dimension=0,
        tiled=True,
    ).astype(jnp.float32)
    norm_second = normed(middle, second_gain).astype(jnp.bfloat16)
    second_all = lax.all_gather(norm_second, "tensor", axis=0, tiled=True)
    gate_pre = jnp.dot(second_all, gate_weight, preferred_element_type=jnp.float32)
    up_proj = jnp.dot(second_all, up_weight, preferred_element_type=jnp.float32)
    activated, gelu_back = jax.vjp(gelu_tanh, gate_pre)
    hidden_low = (activated * up_proj).astype(jnp.bfloat16)
    picked = hidden_low
    layer_out = middle + lax.psum_scatter(
        lax.dot_general(
            picked, down_weight, contract_cols, preferred_element_type=jnp.float32
        ).astype(jnp.bfloat16),
        "tensor",
        scatter_dimension=0,
        tiled=True,
    ).astype(jnp.float32)
    grad_all = lax.all_gather(cotangent, "tensor", axis=0, tiled=True)
    down_grad = lax.dot_general(
        grad_all, hidden_low, contract_rows, preferred_element_type=jnp.float32
    )
    grad_hidden = jnp.dot(grad_all, down_weight, preferred_element_type=jnp.float32)
    (grad_act,) = gelu_back(grad_hidden * up_proj)
    grad_gate_low = grad_act.astype(jnp.bfloat16)
    grad_up_low = (grad_hidden * activated).astype(jnp.bfloat16)
    gate_grad = lax.dot_general(
        second_all, grad_gate_low, contract_rows, preferred_element_type=jnp.float32
    )
    up_grad = lax.dot_general(
        second_all, grad_up_low, contract_rows, preferred_element_type=jnp.float32
    )
    summed_rows = lax.dot_general(
        grad_gate_low, gate_weight, contract_cols, preferred_element_type=jnp.float32
    )
    grad_second = lax.psum_scatter(
        (
            summed_rows
            + lax.dot_general(
                grad_up_low, up_weight, contract_cols, preferred_element_type=jnp.float32
            )
        ).astype(jnp.bfloat16),
        "tensor",
        scatter_dimension=0,
        tiled=True,
    ).astype(jnp.float32)
    _, second_back = jax.vjp(normed, middle, second_gain)
    middle_part, second_gain_grad = second_back(grad_second)
    grad_middle = cotangent.astype(jnp.float32) + middle_part
    middle_all = lax.all_gather(grad_middle.astype(jnp.bfloat16), "tensor", axis=0, tiled=True)
    out_grad = lax.dot_general(
        middle_all, attended_low, contract_rows, preferred_element_type=jnp.float32
    )
    grad_attended = jnp.dot(middle_all, out_weight, preferred_element_type=jnp.float32).astype(
        jnp.bfloat16
    )
    grad_attended = grad_attended.reshape(all_rows, head_count, head_dim)

    def backward_block(block_id, running):
        grad_query, grad_key, grad_value, grad_distance = running
        sequence, query_start, row_start = locate(block_id)
        query_block = lax.dynamic_slice_in_dim(query_heads, row_start, QBLK, 0)
        scores = block_scores(
            query_block, key_heads, distance_bias, piece_start[sequence], query_start
        )
        softmax_rows = jnp.exp(scores - log_norms[block_id][..., None])
        grad_block = lax.dynamic_slice_in_dim(grad_attended, row_start, QBLK, 0)
        grad_probs = jnp.einsum(
            "qhd,khd->hqk", grad_block, value_heads, preferred_element_type=jnp.float32
        )
        weighted = jnp.sum(softmax_rows * grad_probs, axis=-1, keepdims=True)
        grad_scores = (softmax_rows * (grad_probs - weighted)).astype(jnp.bfloat16)
        query_part = jnp.einsum(
            "hqk,khd->qhd", grad_scores, key_heads, preferred_element_type=jnp.float32
        )
        key_part = jnp.einsum(
            "hqk,qhd->khd", grad_scores, query_block, preferred_element_type=jnp.float32
        )
        value_part = jnp.einsum(
            "hqk,qhd->khd",
            softmax_rows.astype(jnp.bfloat16),
            grad_block,
            preferred_element_type=jnp.float32,
        )
        grad_query = lax.dynamic_update_slice_in_dim(grad_query, query_part, row_start, 0)
        grad_key = grad_key + key_part
        grad_value = grad_value + value_part
        diag_part = diagonal_sums(grad_scores.astype(jnp.float32))
        width = QBLK + LEN - 1
        diag_from = LEN - QBLK - query_start
        current = lax.dynamic_slice_in_dim(grad_distance, diag_from, width, 1)
        grad_distance = lax.dynamic_update_slice_in_dim(
            grad_distance, current + diag_part, diag_from, 1
        )
        return (grad_query, grad_key, grad_value, grad_distance)

    zero_heads = jnp.zeros((all_rows, head_count, head_dim), jnp.float32)
    zero_distance = jnp.zeros((head_count, 2 * LEN - 1), jnp.float32)
    grad_query, grad_key, grad_value, grad_distance = lax.fori_loop(
        0, block_count, backward_block, (zero_heads, zero_heads, zero_heads, zero_distance)
    )
    table_grad = jnp.dot(distance_hot.T, grad_distance.T, precision=HIGHEST)
    grad_query_low = grad_query.reshape(all_rows, inner_dev).astype(jnp.bfloat16)
    grad_key_low = grad_key.reshape(all_rows, inner_dev).astype(jnp.bfloat16)
    grad_value_low = grad_value.reshape(all_rows, inner_dev).astype(jnp.bfloat16)
    query_grad = lax.dot_general(
        first_all, grad_query_low, contract_rows, preferred_element_type=jnp.float32
    )
    key_grad = lax.dot_general(
        first_all, grad_key_low, contract_rows, preferred_element_type=jnp.float32
    )
    value_grad = lax.dot_general(
        first_all, grad_value_low, contract_rows, preferred_element_type=jnp.float32
    )
    summed_rows = jnp.zeros(
        (lax.axis_size("tensor") * own_rows, query_weight.shape[0]), jnp.float32
    )
    for grad_low, weight in (
        (grad_query_low, query_weight),
        (grad_key_low, key_weight),
        (grad_value_low, value_weight),
    ):
        picked = grad_low
        summed_rows = summed_rows + lax.dot_general(
            picked, weight, contract_cols, preferred_element_type=jnp.float32
        )
    grad_first = lax.psum_scatter(
        summed_rows.astype(jnp.bfloat16), "tensor", scatter_dimension=0, tiled=True
    ).astype(jnp.float32)
    _, first_back = jax.vjp(normed, inputs, first_gain)
    input_part, first_gain_grad = first_back(grad_first)
    input_grad = grad_middle + input_part
    query_grad, key_grad, value_grad, out_grad, gate_grad, up_grad, down_grad = (
        lax.psum_scatter(query_grad, "dp", scatter_dimension=0, tiled=True),
        lax.psum_scatter(key_grad, "dp", scatter_dimension=0, tiled=True),
        lax.psum_scatter(value_grad, "dp", scatter_dimension=0, tiled=True),
        lax.psum_scatter(out_grad, "dp", scatter_dimension=0, tiled=True),
        lax.psum_scatter(gate_grad, "dp", scatter_dimension=0, tiled=True),
        lax.psum_scatter(up_grad, "dp", scatter_dimension=0, tiled=True),
        lax.psum_scatter(down_grad, "dp", scatter_dimension=0, tiled=True),
    )
    table_grad = lax.psum(table_grad, "dp")
    first_gain_grad, second_gain_grad = lax.psum(
        (first_gain_grad, second_gain_grad), ("dp", "tensor")
    )
    return (
        layer_out.astype(jnp.bfloat16),
        input_grad.astype(jnp.bfloat16),
        first_gain_grad,
        query_grad,
        key_grad,
        value_grad,
        out_grad,
        table_grad,
        second_gain_grad,
        gate_grad,
        up_grad,
        down_grad,
    )


def solution(mesh):
    return jax.shard_map(
        per_device,
        mesh=mesh,
        in_specs=(
            P(("dp", "tensor"), None),
            P(),
            P(None, "tensor"),
            P(None, "tensor"),
            P(None, "tensor"),
            P(None, "tensor"),
            P(None, "tensor"),
            P(),
            P(None, "tensor"),
            P(None, "tensor"),
            P(None, "tensor"),
            P("dp", None),
            P(),
            P(("dp", "tensor"), None),
        ),
        out_specs=(
            P(("dp", "tensor"), None),
            P(("dp", "tensor"), None),
            P(),
            P("dp", "tensor"),
            P("dp", "tensor"),
            P("dp", "tensor"),
            P("dp", "tensor"),
            P(None, "tensor"),
            P(),
            P("dp", "tensor"),
            P("dp", "tensor"),
            P("dp", "tensor"),
        ),
        check_vma=False,
    )
```

profile of v0, /device:TPU:0, one launch (start us, length us, event | category | flops | bytes accessed | tf_op | source)
XLA Modules:
  0.0 1671.4 jit_solution(16654163404661405045)
XLA Ops:
  13.0 65.6 %all-gather.5.cloned.1.call-done = bf16[1024,1536]{1,0:T(8,128)(2,1)} async-done(((bf16[256,1536]{1,0:T(8,128)(2,1)}), bf16[1024,1536]{1,0:T(8,128)(2,1)}) %all-gather.5.cloned.1.call-update) | async-done | bytes 3145744 | tf_op jit(solution)/shard_map/all_gather | solution.py:103
  85.8 241.3 %while.38 = (s32[]{:T(128)}, bf16[2,512,192]{1,2,0:T(8,128)(2,1)}, f32[2,3,512]{2,1,0:T(4,128)}, s32[2]{0:T(128)S(1)}, s32[1,2]{1,0:T(1,128)}, /*index=5*/bf16[1...) while((s32[]{:T(128)}, bf16[2,512,192]{1,2,0:T(8,128)(2,1)}, ...), condition=%wide.region_6.7_spmd, body=%wide.region_1.6_spmd.sunk | while | flops 417348640 | bytes 142808624 | solution.py:132
  97.8 15.2 reshape.403
  113.0 13.8 tile.45
  126.8 11.0 slice.46
  148.9 48.5 %rev.35 = f32[3,512,1024]{2,1,0:T(8,128)} reverse(f32[3,512,1024]{2,1,0:T(8,128)} %slice.47), dimensions={1} | reverse | bytes 12582912 | tf_op jit(solution)/shard_map/while/body/eval_jaxpr/jit(_flip)/rev | solution.py:39
  218.1 15.2 reshape.403
  233.3 13.8 tile.45
  247.1 11.0 slice.46
  258.1 7.6 copy.46
  269.2 48.5 %rev.35 = f32[3,512,1024]{2,1,0:T(8,128)} reverse(f32[3,512,1024]{2,1,0:T(8,128)} %slice.47), dimensions={1} | reverse | bytes 12582912 | tf_op jit(solution)/shard_map/while/body/eval_jaxpr/jit(_flip)/rev | solution.py:39
  332.7 59.0 %reduce-scatter.14.cloned.1.call-done = bf16[256,1536]{1,0:T(8,128)(2,1)} async-done(((bf16[1024,1536]{1,0:T(8,128)(2,1)}), bf16[256,1536]{1,0:T(8,128)(2,1)}) %reduce-scatter.14.cloned.1.call-update) | async-done | bytes 786448 | tf_op jit(solution)/shard_map/reduce_scatter | solution.py:135
  396.6 63.1 %all-gather.7.cloned.1.call-done = bf16[1024,1536]{1,0:T(8,128)(2,1)} async-done(((bf16[256,1536]{1,0:T(8,128)(2,1)}), bf16[1024,1536]{1,0:T(8,128)(2,1)}) %all-gather.7.cloned.1.call-update) | async-done | bytes 3145744 | tf_op jit(solution)/shard_map/all_gather | solution.py:144
  459.7 8.2 fusion.57
  472.9 50.4 %all-gather.9.cloned.1.call-done = bf16[1024,1536]{1,0:T(8,128)(2,1)} async-done(((bf16[256,1536]{1,0:T(8,128)(2,1)}), bf16[1024,1536]{1,0:T(8,128)(2,1)}) %all-gather.9.cloned.1.call-update) | async-done | bytes 3145744 | tf_op jit(solution)/shard_map/all_gather | solution.py:158
  523.3 10.4 multiply_convert_fusion.1
  542.5 59.0 %reduce-scatter.18.cloned.1.call-done = bf16[256,1536]{1,0:T(8,128)(2,1)} async-done(((bf16[1024,1536]{1,0:T(8,128)(2,1)}), bf16[256,1536]{1,0:T(8,128)(2,1)}) %reduce-scatter.18.cloned.1.call-update) | async-done | bytes 786448 | tf_op jit(solution)/shard_map/reduce_scatter | solution.py:175
  607.9 63.6 %all-gather.11.cloned.1.call-done = bf16[1024,1536]{1,0:T(8,128)(2,1)} async-done(((bf16[256,1536]{1,0:T(8,128)(2,1)}), bf16[1024,1536]{1,0:T(8,128)(2,1)}) %all-gather.11.cloned.1.call-update) | async-done | bytes 3145744 | tf_op jit(solution)/shard_map/all_gather | solution.py:189
  676.2 489.1 %while.39 = (s32[]{:T(128)}, bf16[1024,3,64]{0,2,1:T(8,128)(2,1)}, f32[1024,3,64]{0,2,1:T(8,128)}, f32[1024,3,64]{0,2,1:T(8,128)}, f32[3,2047]{1,0:T(4,128)S(1)}...) while((s32[]{:T(128)}, bf16[1024,3,64]{0,2,1:T(8,128)(2,1)}, ...), condition=%wide.region_17.18_spmd.clone, body=%wide.region_12.17_spmd.clone.sunk | while | flops 1026050048 | bytes 305763776 | solution.py:238
  690.6 15.2 reshape.404
  705.8 14.3 tile.47
  720.0 11.0 slice.48
  731.0 7.6 copy.47
  742.1 48.5 %rev.36 = f32[3,512,1024]{2,1,0:T(8,128)} reverse(f32[3,512,1024]{2,1,0:T(8,128)} %slice.49), dimensions={1} | reverse | bytes 12582912 | tf_op jit(solution)/shard_map/while/body/eval_jaxpr/jit(_flip)/rev | solution.py:39
  806.1 46.0 %rev.37 = f32[3,512,1024]{2,1,0:T(8,128)} reverse(bf16[3,512,1024]{2,1,0:T(8,128)(2,1)} %copy-done.1), dimensions={1} | reverse | bytes 9437184 | tf_op jit(solution)/shard_map/while/body/eval_jaxpr/jit(_flip)/rev | solution.py:45
  856.1 19.9 %copy.48 = f32[1,3,512,1536]{3,1,2,0:T(4,128)S(1)} copy(f32[1,3,512,1536]{3,2,1,0:T(8,128)S(1)} %pad_bitcast_fusion.2) | data formatting | bytes 18874368 | tf_op jit(solution)/shard_map/while
  881.0 14.2 reshape.405
  895.2 16.3 reshape.406
  930.8 15.2 reshape.404
  946.0 14.0 tile.47
  959.9 11.0 slice.48
  982.1 48.5 %rev.36 = f32[3,512,1024]{2,1,0:T(8,128)} reverse(f32[3,512,1024]{2,1,0:T(8,128)} %slice.49), dimensions={1} | reverse | bytes 12582912 | tf_op jit(solution)/shard_map/while/body/eval_jaxpr/jit(_flip)/rev | solution.py:39
  1047.1 46.0 %rev.37 = f32[3,512,1024]{2,1,0:T(8,128)} reverse(bf16[3,512,1024]{2,1,0:T(8,128)(2,1)} %copy-done.1), dimensions={1} | reverse | bytes 9437184 | tf_op jit(solution)/shard_map/while/body/eval_jaxpr/jit(_flip)/rev | solution.py:45
  1097.2 19.9 %copy.48 = f32[1,3,512,1536]{3,1,2,0:T(4,128)S(1)} copy(f32[1,3,512,1536]{3,2,1,0:T(8,128)S(1)} %pad_bitcast_fusion.2) | data formatting | bytes 18874368 | tf_op jit(solution)/shard_map/while
  1122.1 14.2 reshape.405
  1136.3 16.5 reshape.406
  1180.8 8.4 convolution_bitcast_fusion.2
  1195.8 8.6 fusion.66
  1204.8 8.6 fusion.65
  1232.0 14.3 psum.22
  1248.3 43.6 %all-reduce.2 = (f32[1536]{0:T(1024)}, f32[1536]{0:T(1024)}) all-reduce(f32[1536]{0:T(1024)S(1)} %get-tuple-element.593, f32[1536]{0:T(1024)S(1)} %copy-done.23), channel_id=1, replica_groups=mesh['dp'=8,'tensor'=4] {'dp','tensor'}, use_global_device_ids=true, to_apply=%region_21.22 | all-reduce | flops 3072 | bytes 24576 | tf_op jit(solution)/shard_map/psum | solution.py:282
  1301.4 61.1 %reduce-scatter.34.cloned.1.call-done = f32[192,992]{1,0:T(8,128)} async-done(((f32[1536,992]{1,0:T(8,128)}), f32[192,992]{1,0:T(8,128)}) %reduce-scatter.34.cloned.1.call-update) | async-done | bytes 761872
  1362.5 65.9 %reduce-scatter.32.cloned.1.call-done = f32[192,992]{1,0:T(8,128)} async-done(((f32[1536,992]{1,0:T(8,128)}), f32[192,992]{1,0:T(8,128)}) %reduce-scatter.32.cloned.1.call-update) | async-done | bytes 761872 | tf_op jit(solution)/shard_map/reduce_scatter | solution.py:278
  1428.4 65.7 %reduce-scatter.30.cloned.1.call-done = f32[192,992]{1,0:T(8,128)} async-done(((f32[1536,992]{1,0:T(8,128)}), f32[192,992]{1,0:T(8,128)}) %reduce-scatter.30.cloned.1.call-update) | async-done | bytes 761872 | tf_op jit(solution)/shard_map/reduce_scatter | solution.py:277
  1494.2 42.5 %reduce-scatter.28.cloned.1.call-done = f32[192,192]{1,0:T(8,128)} async-done(((f32[1536,192]{1,0:T(8,128)}), f32[192,192]{1,0:T(8,128)}) %reduce-scatter.28.cloned.1.call-update) | async-done | bytes 147472 | tf_op jit(solution)/shard_map/reduce_scatter | solution.py:276
  1536.7 42.7 %reduce-scatter.26.cloned.1.call-done = f32[192,192]{1,0:T(8,128)} async-done(((f32[1536,192]{1,0:T(8,128)}), f32[192,192]{1,0:T(8,128)}) %reduce-scatter.26.cloned.1.call-update) | async-done | bytes 147472 | tf_op jit(solution)/shard_map/reduce_scatter | solution.py:275
  1579.4 42.5 %reduce-scatter.22.cloned.1.call-done = f32[192,192]{1,0:T(8,128)} async-done(((f32[1536,192]{1,0:T(8,128)}), f32[192,192]{1,0:T(8,128)}) %reduce-scatter.22.cloned.1.call-update) | async-done | bytes 147472 | tf_op jit(solution)/shard_map/reduce_scatter | solution.py:273
  1621.9 42.5 %reduce-scatter.24.cloned.1.call-done = f32[192,192]{1,0:T(8,128)} async-done(((f32[1536,192]{1,0:T(8,128)}), f32[192,192]{1,0:T(8,128)}) %reduce-scatter.24.cloned.1.call-update) | async-done | bytes 147472 | tf_op jit(solution)/shard_map/reduce_scatter | solution.py:274
  (259 shorter events, 253.7 us)
Async XLA Ops:
  7.2 516.1 %copy-start = (bf16[1536,992]{0,1:T(8,128)(2,1)S(1)}, bf16[1536,992]{0,1:T(8,128)(2,1)}, u32[]{:S(2)}) copy-start(bf16[1536,992]{0,1:T(8,128)(2,1)} %param.28) | copy-start | bytes 9142276
  7.2 5.1 copy-start.37
  7.2 5.1 copy-start.39
  7.2 71.3 %all-gather.5.cloned.1.call-start = ((), (), s32[]{:S(2)}) async-start(), calls=%async_computation.11 | async-start | bytes 3932160 | tf_op jit(solution)/shard_map/all_gather | solution.py:103
  12.2 379.5 %reduce-scatter.14.cloned.1.call-start = ((), (), s32[]{:S(2)}) async-start(), calls=%async_computation.12 | async-start | bytes 3932160 | tf_op jit(solution)/shard_map/reduce_scatter | solution.py:135
  78.6 4.1 copy-start.16
  78.6 4.1 copy-start.32
  323.5 2.3 copy-start.18
  332.6 60.8 %copy-start.20 = (f32[1536]{0:T(1024)S(1)}, f32[1536]{0:T(1024)}, u32[]{:S(2)}) copy-start(f32[1536]{0:T(1024)} %param.25) | copy-start | bytes 18436
  332.6 127.0 %all-gather.7.cloned.1.call-start = ((), (), s32[]{:S(2)}) async-start(), calls=%async_computation.13 | async-start | bytes 3932160 | tf_op jit(solution)/shard_map/all_gather | solution.py:144
  393.4 211.0 %copy-start.24 = (f32[256]{0:T(256)}, f32[256]{0:T(256)S(1)}, u32[]{:S(2)}) copy-start(f32[256]{0:T(256)S(1)} %fusion.53) | copy-start | bytes 3076
  396.0 127.3 %all-gather.9.cloned.1.call-start = ((), (), s32[]{:S(2)}) async-start(), calls=%async_computation.15 | async-start | bytes 3932160 | tf_op jit(solution)/shard_map/all_gather | solution.py:158
  396.6 204.9 %reduce-scatter.18.cloned.1.call-start = ((), (), s32[]{:S(2)}) async-start(), calls=%async_computation.16 | async-start | bytes 3932160 | tf_op jit(solution)/shard_map/reduce_scatter | solution.py:175
  459.7 8.2 copy-start.33
  459.7 8.2 copy-start.34
  523.3 10.4 copy-start.35
  533.7 3.5 copy-start.40
  533.7 3.5 copy-start.41
  533.7 3.5 copy-start.36
  542.4 129.0 %all-gather.11.cloned.1.call-start = ((), (), s32[]{:S(2)}) async-start(), calls=%async_computation.17 | async-start | bytes 3932160 | tf_op jit(solution)/shard_map/all_gather | solution.py:189
  604.4 71.0 %copy-start.30 = (f32[256]{0:T(256)}, f32[256]{0:T(256)S(1)}, u32[]{:S(2)}) copy-start(f32[256]{0:T(256)S(1)} %multiply_multiply_fusion.4) | copy-start | bytes 3076
  607.8 638.4 %reduce-scatter.20.cloned.1.call-start = ((), (), s32[]{:S(2)}) async-start(), calls=%async_computation.18 | async-start | bytes 3932160 | tf_op jit(solution)/shard_map/reduce_scatter | solution.py:266
  796.7 4.0 copy-start.2
  796.8 4.0 copy-start.5
  800.7 3.0 copy-start.1
  1036.7 4.0 copy-start.2
  1036.7 4.0 copy-start.5
  1040.7 3.0 copy-start.1
  1166.5 3.7 copy-start.12
  1167.8 3.4 copy-start.13
  1167.8 2.4 copy-start.17
  1174.1 122.7 %reduce-scatter.16.cloned.1.call-start = ((), (), s32[]{:S(2)}) async-start(), calls=%async_computation.14 | async-start | bytes 3932160 | tf_op jit(solution)/shard_map/reduce_scatter | solution.py:150
  1180.7 181.8 %reduce-scatter.34.cloned.1.call-start = ((), (), s32[]{:S(2)}) async-start(), calls=%async_computation.25 | async-start | bytes 7077888
  1195.8 232.7 %reduce-scatter.32.cloned.1.call-start = ((), (), s32[]{:S(2)}) async-start(), calls=%async_computation.24 | async-start | bytes 7077888 | tf_op jit(solution)/shard_map/reduce_scatter | solution.py:278
  1204.5 289.7 %reduce-scatter.30.cloned.1.call-start = ((), (), s32[]{:S(2)}) async-start(), calls=%async_computation.23 | async-start | bytes 7077888 | tf_op jit(solution)/shard_map/reduce_scatter | solution.py:277
  1213.4 323.3 %reduce-scatter.28.cloned.1.call-start = ((), (), s32[]{:S(2)}) async-start(), calls=%async_computation.22 | async-start | bytes 1769472 | tf_op jit(solution)/shard_map/reduce_scatter | solution.py:276
  1218.5 4.4 copy-start.11
  1218.5 360.9 %reduce-scatter.26.cloned.1.call-start = ((), (), s32[]{:S(2)}) async-start(), calls=%async_computation.21 | async-start | bytes 1769472 | tf_op jit(solution)/shard_map/reduce_scatter | solution.py:275
  1222.8 399.1 %reduce-scatter.22.cloned.1.call-start = ((), (), s32[]{:S(2)}) async-start(), calls=%async_computation.19 | async-start | bytes 1769472 | tf_op jit(solution)/shard_map/reduce_scatter | solution.py:273
  1227.0 4.4 copy-start.38
  1227.0 19.2 %copy-start.22 = (f32[1536]{0:T(1024)S(1)}, f32[1536]{0:T(1024)}, u32[]{:S(2)}) copy-start(f32[1536]{0:T(1024)} %param.19) | copy-start | bytes 18436
  1227.0 19.2 %copy-start.27 = (f32[256]{0:T(256)S(1)}, f32[256]{0:T(256)}, u32[]{:S(2)}) copy-start(f32[256]{0:T(256)} %copy-done.26) | copy-start | bytes 3076
  1227.0 437.4 %reduce-scatter.24.cloned.1.call-start = ((), (), s32[]{:S(2)}) async-start(), calls=%async_computation.20 | async-start | bytes 1769472 | tf_op jit(solution)/shard_map/reduce_scatter | solution.py:274
  1231.3 17.0 %copy-start.23 = (f32[1536]{0:T(1024)S(1)}, f32[1536]{0:T(1024)}, u32[]{:S(2)}) copy-start(f32[1536]{0:T(1024)} %get-tuple-element.591) | copy-start | bytes 18436
  1231.3 60.6 %copy-start.29 = (f32[256]{0:T(256)S(1)}, f32[256]{0:T(256)}, u32[]{:S(2)}) copy-start(f32[256]{0:T(256)} %copy-done.28) | copy-start | bytes 3076
  1231.3 65.5 %copy-start.21 = (f32[1536]{0:T(1024)S(1)}, f32[1536]{0:T(1024)}, u32[]{:S(2)}) copy-start(f32[1536]{0:T(1024)} %param.25) | copy-start | bytes 18436
  1231.3 65.5 %copy-start.25 = (f32[256]{0:T(256)S(1)}, f32[256]{0:T(256)}, u32[]{:S(2)}) copy-start(f32[256]{0:T(256)} %copy-done.24) | copy-start | bytes 3076
  1231.3 65.4 %copy-start.31 = (f32[256]{0:T(256)S(1)}, f32[256]{0:T(256)}, u32[]{:S(2)}) copy-start(f32[256]{0:T(256)} %copy-done.30) | copy-start | bytes 3076
  (19 other events, 23.2 us)
Sparse Core Ops, SparseCore 0:
  12.3 66.1 all-gather.4
  332.7 58.8 reduce-scatter.13
  396.1 63.5 all-gather.6
  461.1 62.1 all-gather.8
  542.6 58.8 reduce-scatter.17
  607.9 63.5 all-gather.10
  1174.2 58.8 reduce-scatter.19
  1235.4 61.3 reduce-scatter.15
  1300.7 61.7 reduce-scatter.33
  1366.7 61.7 reduce-scatter.31
  1432.4 61.7 reduce-scatter.29
  1498.3 38.4 reduce-scatter.27
  1540.9 38.4 reduce-scatter.25
  1583.5 38.4 reduce-scatter.21
  1626.0 38.4 reduce-scatter.23
where the time goes:
time: 1700 us; the launch traced here: 1670 us
  waiting for transfers between devices  729 us (43%)
  local copies, waits for them, and re-layouts  650 us (38%)
  matrix products  145 us (9%)
  other arithmetic  58.7 us (3%)
  blocking collectives  57.9 us (3%)
    rev x4, local copies, waits for them, and re-layouts, bias_rows(): return jnp.flip(skewed, axis=1)  194 us
    while x54, local copies, waits for them, and re-layouts  172 us
    rev x2, local copies, waits for them, and re-layouts, diagonal_sums(): flipped = jnp.flip(grad_block, axis=1)  92 us
    another operation x8, local copies, waits for them, and re-layouts, bias_rows(): tiled = jnp.tile(window, (1, QBLK + 1))[:, :QBLK * (width + 1)]  75.5 us
    reduce_scatter x1, waiting for transfers between devices, per_device(): lax.psum_scatter(up_grad, 'dp', scatter_dimension=0, tiled=True)  65.9 us
    reduce_scatter x1, waiting for transfers between devices, per_device(): lax.psum_scatter(gate_grad, 'dp', scatter_dimension=0, tiled=True)  65.7 us
    all_gather x1, waiting for transfers between devices, per_device(): first_all = lax.all_gather(norm_first, 'tensor', axis=0, tiled=True)  65.6 us
    all_gather x1, waiting for transfers between devices, per_device(): lax.all_gather(grad_middle.astype(jnp.bfloat16), 'tensor', axis=0, tiled=...  63.6 us
  transfers between devices with their start and end apart: 15, of which 14 were waited for; matrix products, arithmetic and copies ran while one was open for 5% of the time, Pallas kernels for 0%

commit v1 on v0

--- a/solution.py
+++ b/solution.py
@@ -155,7 +155,14 @@
         scatter_dimension=0,
         tiled=True,
     ).astype(jnp.float32)
-    grad_all = lax.all_gather(cotangent, "tensor", axis=0, tiled=True)
+    ring = [cotangent]
+    for hop in range(3):
+        ring.append(lax.ppermute(ring[-1], "tensor", [(dev, (dev + 1) % 4) for dev in range(4)]))
+    grad_all = jnp.roll(
+        jnp.concatenate(ring[::-1], axis=0),
+        (lax.axis_index("tensor") + 1) * ring[0].shape[0],
+        axis=0,
+    )
     down_grad = lax.dot_general(
         grad_all, hidden_low, contract_rows, preferred_element_type=jnp.float32
     )

time: 1700 us -> 1700 us (level)
  starting transfers between devices: 0.87 us -> 25.1 us
  waiting for transfers between devices: 729 us -> 705 us
    ppermute x0 -> x3, waiting for transfers between devices: none -> 81 us  [per_device(): lax.ppermute(ring[-1], 'tensor', [(dev, (dev + 1) % 4) for dev in range(4)])]
    all_gather x1, waiting for transfers between devices: 63.1 us -> 0.01 us  [per_device(): second_all = lax.all_gather(norm_second, 'tensor', axis=0, tiled=True)]
    unnamed x16 -> x14, waiting for transfers between devices: 61.8 us -> 0.23 us
    reduce_scatter x0 -> x1, waiting for transfers between devices: none -> 61.2 us  [per_device(): lax.psum_scatter(down_grad, 'dp', scatter_dimension=0, tiled=True)]
    all_gather x1 -> x0, waiting for transfers between devices: 50.4 us -> none  [per_device(): grad_all = lax.all_gather(cotangent, 'tensor', axis=0, tiled=True)]
    ppermute x0 -> x3, starting transfers between devices: none -> 24.2 us  [per_device(): lax.ppermute(ring[-1], 'tensor', [(dev, (dev + 1) % 4) for dev in range(4)])]
  transfers between devices with their start and end apart: 15 -> 17, of which waited for: 14 -> 15; matrix products, arithmetic and copies ran while one was open for 5% -> 4% of each run, Pallas kernels for 0% -> 0%
where the time goes in v1:
time: 1700 us; the launch traced here: 1670 us
  waiting for transfers between devices  705 us (41%)
  local copies, waits for them, and re-layouts  656 us (39%)
  matrix products  141 us (8%)
  other arithmetic  59 us (3%)
  blocking collectives  56 us (3%)
  starting transfers between devices  25.1 us (1%)
    rev x4, local copies, waits for them, and re-layouts, bias_rows(): return jnp.flip(skewed, axis=1)  194 us
    while x54, local copies, waits for them, and re-layouts  172 us
    rev x2, local copies, waits for them, and re-layouts, diagonal_sums(): flipped = jnp.flip(grad_block, axis=1)  91.9 us
    ppermute x3, waiting for transfers between devices, per_device(): lax.ppermute(ring[-1], 'tensor', [(dev, (dev + 1) % 4) for dev in range(4)])  81 us
    another operation x8, local copies, waits for them, and re-layouts, bias_rows(): tiled = jnp.tile(window, (1, QBLK + 1))[:, :QBLK * (width + 1)]  75.5 us
    reduce_scatter x1, waiting for transfers between devices, per_device(): lax.psum_scatter(up_grad, 'dp', scatter_dimension=0, tiled=True)  66.1 us
    reduce_scatter x1, waiting for transfers between devices, per_device(): lax.psum_scatter(gate_grad, 'dp', scatter_dimension=0, tiled=True)  65.6 us
    all_gather x1, waiting for transfers between devices, per_device(): first_all = lax.all_gather(norm_first, 'tensor', axis=0, tiled=True)  65.6 us
  transfers between devices with their start and end apart: 17, of which 15 were waited for; matrix products, arithmetic and copies ran while one was open for 4% of the time, Pallas kernels for 0%

profile of v1, /device:TPU:0, one launch (start us, length us, event | category | flops | bytes accessed | tf_op | source)
XLA Modules:
  0.0 1672.7 jit_solution(3331185454591609009)
XLA Ops:
  12.9 65.6 %all-gather.4.cloned.1.call-done = bf16[1024,1536]{1,0:T(8,128)(2,1)} async-done(((bf16[256,1536]{1,0:T(8,128)(2,1)}), bf16[1024,1536]{1,0:T(8,128)(2,1)}) %all-gather.4.cloned.1.call-update) | async-done | bytes 3145744 | tf_op jit(solution)/shard_map/all_gather | solution.py:103
  85.7 241.1 %while.38 = (s32[]{:T(128)}, bf16[2,512,192]{1,2,0:T(8,128)(2,1)}, f32[2,3,512]{2,1,0:T(4,128)}, s32[2]{0:T(128)S(1)}, s32[1,2]{1,0:T(1,128)}, /*index=5*/bf16[1...) while((s32[]{:T(128)}, bf16[2,512,192]{1,2,0:T(8,128)(2,1)}, ...), condition=%wide.region_6.7_spmd, body=%wide.region_1.6_spmd.sunk | while | flops 417348640 | bytes 142808624 | solution.py:132
  97.7 15.2 reshape.401
  112.9 13.8 tile.45
  126.7 11.0 slice.46
  148.8 48.4 %rev.35 = f32[3,512,1024]{2,1,0:T(8,128)} reverse(f32[3,512,1024]{2,1,0:T(8,128)} %slice.47), dimensions={1} | reverse | bytes 12582912 | tf_op jit(solution)/shard_map/while/body/eval_jaxpr/jit(_flip)/rev | solution.py:39
  218.0 15.2 reshape.401
  233.1 13.8 tile.45
  246.9 11.0 slice.46
  269.0 48.4 %rev.35 = f32[3,512,1024]{2,1,0:T(8,128)} reverse(f32[3,512,1024]{2,1,0:T(8,128)} %slice.47), dimensions={1} | reverse | bytes 12582912 | tf_op jit(solution)/shard_map/while/body/eval_jaxpr/jit(_flip)/rev | solution.py:39
  332.5 59.0 %reduce-scatter.12.cloned.1.call-done = bf16[256,1536]{1,0:T(8,128)(2,1)} async-done(((bf16[1024,1536]{1,0:T(8,128)(2,1)}), bf16[256,1536]{1,0:T(8,128)(2,1)}) %reduce-scatter.12.cloned.1.call-update) | async-done | bytes 786448 | tf_op jit(solution)/shard_map/reduce_scatter | solution.py:135
  396.9 29.9 %collective-permute-done = bf16[256,1536]{1,0:T(8,128)(2,1)S(1)} collective-permute-done((bf16[256,1536]{1,0:T(8,128)(2,1)}, bf16[256,1536]{1,0:T(8,128)(2,1)S(1)}, u32[]{:S(2)}, u32[]{:S(2)}) %collective-permute-start) | collective-permute-done | bytes 786464 | tf_op jit(solution)/shard_map/ppermute | solution.py:160
  427.7 10.9 collective-permute-start.1
  438.6 32.5 %collective-permute-done.1 = bf16[256,1536]{1,0:T(8,128)(2,1)} collective-permute-done((bf16[256,1536]{1,0:T(8,128)(2,1)S(1)}, bf16[256,1536]{1,0:T(8,128)(2,1)}, u32[]{:S(2)}, u32[]{:S(2)}) %collective-permute-start.1) | collective-permute-done | bytes 786464 | tf_op jit(solution)/shard_map/ppermute | solution.py:160
  471.0 12.3 collective-permute-start.2
  483.4 18.6 %collective-permute-done.2 = bf16[256,1536]{1,0:T(8,128)(2,1)} collective-permute-done((bf16[256,1536]{1,0:T(8,128)(2,1)}, bf16[256,1536]{1,0:T(8,128)(2,1)}, u32[]{:S(2)}, u32[]{:S(2)}) %collective-permute-start.2) | collective-permute-done | bytes 786464 | tf_op jit(solution)/shard_map/ppermute | solution.py:160
  523.8 9.3 multiply_convert_fusion.1
  541.9 59.9 %reduce-scatter.16.cloned.1.call-done = bf16[256,1536]{1,0:T(8,128)(2,1)} async-done(((bf16[1024,1536]{1,0:T(8,128)(2,1)}), bf16[256,1536]{1,0:T(8,128)(2,1)}) %reduce-scatter.16.cloned.1.call-update) | async-done | bytes 786448 | tf_op jit(solution)/shard_map/reduce_scatter | solution.py:182
  608.2 63.6 %all-gather.8.cloned.1.call-done = bf16[1024,1536]{1,0:T(8,128)(2,1)} async-done(((bf16[256,1536]{1,0:T(8,128)(2,1)}), bf16[1024,1536]{1,0:T(8,128)(2,1)}) %all-gather.8.cloned.1.call-update) | async-done | bytes 3145744 | tf_op jit(solution)/shard_map/all_gather | solution.py:196
  676.6 489.7 %while.39 = (s32[]{:T(128)}, bf16[1024,3,64]{0,2,1:T(8,128)(2,1)}, f32[1024,3,64]{0,2,1:T(8,128)}, f32[1024,3,64]{0,2,1:T(8,128)}, f32[3,2047]{1,0:T(4,128)S(1)}...) while((s32[]{:T(128)}, bf16[1024,3,64]{0,2,1:T(8,128)(2,1)}, ...), condition=%wide.region_17.18_spmd.clone, body=%wide.region_12.17_spmd.clone.sunk | while | flops 1026050048 | bytes 305763776 | solution.py:245
  690.9 15.2 reshape.402
  706.1 14.3 tile.47
  720.4 11.0 slice.48
  742.5 48.4 %rev.36 = f32[3,512,1024]{2,1,0:T(8,128)} reverse(f32[3,512,1024]{2,1,0:T(8,128)} %slice.49), dimensions={1} | reverse | bytes 12582912 | tf_op jit(solution)/shard_map/while/body/eval_jaxpr/jit(_flip)/rev | solution.py:39
  806.4 45.9 %rev.37 = f32[3,512,1024]{2,1,0:T(8,128)} reverse(bf16[3,512,1024]{2,1,0:T(8,128)(2,1)} %copy-done.1), dimensions={1} | reverse | bytes 9437184 | tf_op jit(solution)/shard_map/while/body/eval_jaxpr/jit(_flip)/rev | solution.py:45
  856.3 19.9 %copy.41 = f32[1,3,512,1536]{3,1,2,0:T(4,128)S(1)} copy(f32[1,3,512,1536]{3,2,1,0:T(8,128)S(1)} %pad_bitcast_fusion.2) | data formatting | bytes 18874368 | tf_op jit(solution)/shard_map/while
  881.3 14.2 reshape.403
  895.4 16.3 reshape.404
  931.1 15.2 reshape.402
  946.2 14.0 tile.47
  960.2 11.0 slice.48
  982.3 48.4 %rev.36 = f32[3,512,1024]{2,1,0:T(8,128)} reverse(f32[3,512,1024]{2,1,0:T(8,128)} %slice.49), dimensions={1} | reverse | bytes 12582912 | tf_op jit(solution)/shard_map/while/body/eval_jaxpr/jit(_flip)/rev | solution.py:39
  1047.4 45.9 %rev.37 = f32[3,512,1024]{2,1,0:T(8,128)} reverse(bf16[3,512,1024]{2,1,0:T(8,128)(2,1)} %copy-done.1), dimensions={1} | reverse | bytes 9437184 | tf_op jit(solution)/shard_map/while/body/eval_jaxpr/jit(_flip)/rev | solution.py:45
  1097.3 19.9 %copy.41 = f32[1,3,512,1536]{3,1,2,0:T(4,128)S(1)} copy(f32[1,3,512,1536]{3,2,1,0:T(8,128)S(1)} %pad_bitcast_fusion.2) | data formatting | bytes 18874368 | tf_op jit(solution)/shard_map/while
  1122.3 14.2 reshape.403
  1136.5 16.5 reshape.404
  1181.8 8.7 fusion.36
  1190.5 8.7 fusion.72
  1226.9 14.5 psum.22
  1243.7 41.6 %all-reduce.2 = (f32[1536]{0:T(1024)}, f32[1536]{0:T(1024)}) all-reduce(f32[1536]{0:T(1024)S(1)} %get-tuple-element.545, f32[1536]{0:T(1024)S(1)} %copy-done.26), channel_id=1, replica_groups=mesh['dp'=8,'tensor'=4] {'dp','tensor'}, use_global_device_ids=true, to_apply=%region_21.22 | all-reduce | flops 3072 | bytes 24576 | tf_op jit(solution)/shard_map/psum | solution.py:289
  1285.3 12.3 reduce-scatter.14.cloned.1.call-done
  1302.3 61.2 %reduce-scatter.32.cloned.1.call-done = f32[192,992]{1,0:T(8,128)} async-done(((f32[1536,992]{1,0:T(8,128)}), f32[192,992]{1,0:T(8,128)}) %reduce-scatter.32.cloned.1.call-update) | async-done | bytes 761872 | tf_op jit(solution)/shard_map/reduce_scatter | solution.py:286
  1363.5 66.1 %reduce-scatter.30.cloned.1.call-done = f32[192,992]{1,0:T(8,128)} async-done(((f32[1536,992]{1,0:T(8,128)}), f32[192,992]{1,0:T(8,128)}) %reduce-scatter.30.cloned.1.call-update) | async-done | bytes 761872 | tf_op jit(solution)/shard_map/reduce_scatter | solution.py:285
  1429.6 65.6 %reduce-scatter.28.cloned.1.call-done = f32[192,992]{1,0:T(8,128)} async-done(((f32[1536,992]{1,0:T(8,128)}), f32[192,992]{1,0:T(8,128)}) %reduce-scatter.28.cloned.1.call-update) | async-done | bytes 761872 | tf_op jit(solution)/shard_map/reduce_scatter | solution.py:284
  1495.2 42.7 %reduce-scatter.26.cloned.1.call-done = f32[192,192]{1,0:T(8,128)} async-done(((f32[1536,192]{1,0:T(8,128)}), f32[192,192]{1,0:T(8,128)}) %reduce-scatter.26.cloned.1.call-update) | async-done | bytes 147472 | tf_op jit(solution)/shard_map/reduce_scatter | solution.py:283
  1537.9 42.6 %reduce-scatter.24.cloned.1.call-done = f32[192,192]{1,0:T(8,128)} async-done(((f32[1536,192]{1,0:T(8,128)}), f32[192,192]{1,0:T(8,128)}) %reduce-scatter.24.cloned.1.call-update) | async-done | bytes 147472 | tf_op jit(solution)/shard_map/reduce_scatter | solution.py:282
  1580.4 42.7 %reduce-scatter.20.cloned.1.call-done = f32[192,192]{1,0:T(8,128)} async-done(((f32[1536,192]{1,0:T(8,128)}), f32[192,192]{1,0:T(8,128)}) %reduce-scatter.20.cloned.1.call-update) | async-done | bytes 147472 | tf_op jit(solution)/shard_map/reduce_scatter | solution.py:280
  1623.1 42.6 %reduce-scatter.22.cloned.1.call-done = f32[192,192]{1,0:T(8,128)} async-done(((f32[1536,192]{1,0:T(8,128)}), f32[192,192]{1,0:T(8,128)}) %reduce-scatter.22.cloned.1.call-update) | async-done | bytes 147472 | tf_op jit(solution)/shard_map/reduce_scatter | solution.py:281
  (273 shorter events, 284.8 us)
Async XLA Ops:
  7.2 516.6 %copy-start = (bf16[1536,992]{0,1:T(8,128)(2,1)S(1)}, bf16[1536,992]{0,1:T(8,128)(2,1)}, u32[]{:S(2)}) copy-start(bf16[1536,992]{0,1:T(8,128)(2,1)} %param.28) | copy-start | bytes 9142276
  7.2 5.0 copy-start.39
  7.2 5.0 copy-start.41
  7.2 71.3 %all-gather.4.cloned.1.call-start = ((), (), s32[]{:S(2)}) async-start(), calls=%async_computation.11 | async-start | bytes 3932160 | tf_op jit(solution)/shard_map/all_gather | solution.py:103
  12.1 379.3 %reduce-scatter.12.cloned.1.call-start = ((), (), s32[]{:S(2)}) async-start(), calls=%async_computation.12 | async-start | bytes 3932160 | tf_op jit(solution)/shard_map/reduce_scatter | solution.py:135
  78.5 4.1 copy-start.19
  78.5 4.1 copy-start.35
  332.4 60.8 %copy-start.23 = (f32[1536]{0:T(1024)S(1)}, f32[1536]{0:T(1024)}, u32[]{:S(2)}) copy-start(f32[1536]{0:T(1024)} %param.25) | copy-start | bytes 18436
  332.4 181.7 %all-gather.6.cloned.1.call-start = ((), (), s32[]{:S(2)}) async-start(), calls=%async_computation.13 | async-start | bytes 3932160 | tf_op jit(solution)/shard_map/all_gather | solution.py:144
  393.2 211.6 %copy-start.27 = (f32[256]{0:T(256)}, f32[256]{0:T(256)S(1)}, u32[]{:S(2)}) copy-start(f32[256]{0:T(256)S(1)} %fusion.57) | copy-start | bytes 3076
  395.8 206.1 %reduce-scatter.16.cloned.1.call-start = ((), (), s32[]{:S(2)}) async-start(), calls=%async_computation.15 | async-start | bytes 3932160 | tf_op jit(solution)/shard_map/reduce_scatter | solution.py:182
  395.8 31.0 %collective-permute-start = (bf16[256,1536]{1,0:T(8,128)(2,1)}, bf16[256,1536]{1,0:T(8,128)(2,1)S(1)}, u32[]{:S(2)}, u32[]{:S(2)}) collective-permute-start(bf16[256,1536]{1,0:T(8,128)(2,1)} %param.31), channel_id=1, source_target_pairs={{0,1},{1,2},{2,3},{3,0},{4,5},{5,6},{6,7},{7,4},{8,9},{9,10},{10,1... | collective-permute-start | bytes 2359304 | tf_op jit(solution)/shard_map/ppermute | solution.py:160
  427.7 43.4 %collective-permute-start.1 = (bf16[256,1536]{1,0:T(8,128)(2,1)S(1)}, bf16[256,1536]{1,0:T(8,128)(2,1)}, u32[]{:S(2)}, u32[]{:S(2)}) collective-permute-start(bf16[256,1536]{1,0:T(8,128)(2,1)S(1)} %collective-permute-done), channel_id=1, source_target_pairs={{0,1},{1,2},{2,3},{3,0},{4,5},{5,6},{6,7},{7,4},{8,9},{9,10},{10,1... | collective-permute-start | bytes 2359304 | tf_op jit(solution)/shard_map/ppermute | solution.py:160
  471.0 30.9 %collective-permute-start.2 = (bf16[256,1536]{1,0:T(8,128)(2,1)}, bf16[256,1536]{1,0:T(8,128)(2,1)}, u32[]{:S(2)}, u32[]{:S(2)}) collective-permute-start(bf16[256,1536]{1,0:T(8,128)(2,1)} %collective-permute-done.1), channel_id=1, source_target_pairs={{0,1},{1,2},{2,3},{3,0},{4,5},{5,6},{6,7},{7,4},{8,9},{9,10},{10,1... | collective-permute-start | bytes 2359304 | tf_op jit(solution)/shard_map/ppermute | solution.py:160
  483.4 22.7 %copy-start.9 = (bf16[256,1536]{1,0:T(8,128)(2,1)S(1)}, bf16[256,1536]{1,0:T(8,128)(2,1)}, u32[]{:S(2)}) copy-start(bf16[256,1536]{1,0:T(8,128)(2,1)} %copy-done.8) | copy-start | bytes 2359300
  483.4 23.7 %copy-start.5 = (bf16[256,1536]{1,0:T(8,128)(2,1)S(1)}, bf16[256,1536]{1,0:T(8,128)(2,1)}, u32[]{:S(2)}) copy-start(bf16[256,1536]{1,0:T(8,128)(2,1)} %param.31) | copy-start | bytes 2359300
  514.1 6.3 copy-start.36
  514.1 6.3 copy-start.37
  533.1 3.5 copy-start.42
  533.1 3.5 copy-start.43
  533.1 3.5 copy-start.38
  541.9 129.9 %all-gather.8.cloned.1.call-start = ((), (), s32[]{:S(2)}) async-start(), calls=%async_computation.16 | async-start | bytes 3932160 | tf_op jit(solution)/shard_map/all_gather | solution.py:196
  604.8 71.0 %copy-start.33 = (f32[256]{0:T(256)}, f32[256]{0:T(256)S(1)}, u32[]{:S(2)}) copy-start(f32[256]{0:T(256)S(1)} %multiply_multiply_fusion.4) | copy-start | bytes 3076
  608.2 633.2 %reduce-scatter.18.cloned.1.call-start = ((), (), s32[]{:S(2)}) async-start(), calls=%async_computation.17 | async-start | bytes 3932160 | tf_op jit(solution)/shard_map/reduce_scatter | solution.py:273
  797.1 4.0 copy-start.2
  797.1 4.0 copy-start.6
  801.1 3.0 copy-start.1
  1036.9 4.0 copy-start.2
  1036.9 4.0 copy-start.6
  1167.4 3.7 copy-start.15
  1168.8 3.4 copy-start.16
  1175.0 122.6 %reduce-scatter.14.cloned.1.call-start = ((), (), s32[]{:S(2)}) async-start(), calls=%async_computation.14 | async-start | bytes 3932160 | tf_op jit(solution)/shard_map/reduce_scatter | solution.py:150
  1181.7 181.8 %reduce-scatter.32.cloned.1.call-start = ((), (), s32[]{:S(2)}) async-start(), calls=%async_computation.24 | async-start | bytes 7077888 | tf_op jit(solution)/shard_map/reduce_scatter | solution.py:286
  1190.5 239.1 %reduce-scatter.30.cloned.1.call-start = ((), (), s32[]{:S(2)}) async-start(), calls=%async_computation.23 | async-start | bytes 7077888 | tf_op jit(solution)/shard_map/reduce_scatter | solution.py:285
  1199.2 295.9 %reduce-scatter.28.cloned.1.call-start = ((), (), s32[]{:S(2)}) async-start(), calls=%async_computation.22 | async-start | bytes 7077888 | tf_op jit(solution)/shard_map/reduce_scatter | solution.py:284
  1208.2 329.7 %reduce-scatter.26.cloned.1.call-start = ((), (), s32[]{:S(2)}) async-start(), calls=%async_computation.21 | async-start | bytes 1769472 | tf_op jit(solution)/shard_map/reduce_scatter | solution.py:283
  1213.4 4.4 copy-start.14
  1213.4 367.1 %reduce-scatter.24.cloned.1.call-start = ((), (), s32[]{:S(2)}) async-start(), calls=%async_computation.20 | async-start | bytes 1769472 | tf_op jit(solution)/shard_map/reduce_scatter | solution.py:282
  1217.8 405.4 %reduce-scatter.20.cloned.1.call-start = ((), (), s32[]{:S(2)}) async-start(), calls=%async_computation.18 | async-start | bytes 1769472 | tf_op jit(solution)/shard_map/reduce_scatter | solution.py:280
  1221.9 4.3 copy-start.40
  1221.9 19.4 %copy-start.25 = (f32[1536]{0:T(1024)S(1)}, f32[1536]{0:T(1024)}, u32[]{:S(2)}) copy-start(f32[1536]{0:T(1024)} %param.19) | copy-start | bytes 18436
  1221.9 19.4 %copy-start.30 = (f32[256]{0:T(256)S(1)}, f32[256]{0:T(256)}, u32[]{:S(2)}) copy-start(f32[256]{0:T(256)} %copy-done.29) | copy-start | bytes 3076
  1221.9 443.7 %reduce-scatter.22.cloned.1.call-start = ((), (), s32[]{:S(2)}) async-start(), calls=%async_computation.19 | async-start | bytes 1769472 | tf_op jit(solution)/shard_map/reduce_scatter | solution.py:281
  1226.2 17.5 %copy-start.26 = (f32[1536]{0:T(1024)S(1)}, f32[1536]{0:T(1024)}, u32[]{:S(2)}) copy-start(f32[1536]{0:T(1024)} %get-tuple-element.543) | copy-start | bytes 18436
  1226.2 59.1 %copy-start.32 = (f32[256]{0:T(256)S(1)}, f32[256]{0:T(256)}, u32[]{:S(2)}) copy-start(f32[256]{0:T(256)} %copy-done.31) | copy-start | bytes 3076
  1226.2 71.4 %copy-start.24 = (f32[1536]{0:T(1024)S(1)}, f32[1536]{0:T(1024)}, u32[]{:S(2)}) copy-start(f32[1536]{0:T(1024)} %param.25) | copy-start | bytes 18436
  1226.2 71.4 %copy-start.28 = (f32[256]{0:T(256)S(1)}, f32[256]{0:T(256)}, u32[]{:S(2)}) copy-start(f32[256]{0:T(256)} %copy-done.27) | copy-start | bytes 3076
  1226.2 71.4 %copy-start.34 = (f32[256]{0:T(256)S(1)}, f32[256]{0:T(256)}, u32[]{:S(2)}) copy-start(f32[256]{0:T(256)} %copy-done.33) | copy-start | bytes 3076
  (23 other events, 31.7 us)
Sparse Core Ops, SparseCore 0:
  12.3 66.1 all-gather.3
  332.5 58.8 reduce-scatter.11
  395.9 89.0 all-gather.5
  542.0 59.8 reduce-scatter.15
  608.3 63.5 all-gather.7
  1175.1 58.8 reduce-scatter.17
  1236.4 61.2 reduce-scatter.13
  1301.6 61.8 reduce-scatter.31
  1367.8 61.7 reduce-scatter.29
  1433.4 61.7 reduce-scatter.27
  1499.4 38.4 reduce-scatter.25
  1541.9 38.4 reduce-scatter.23
  1584.7 38.4 reduce-scatter.19
  1627.2 38.4 reduce-scatter.21
